TPU v7x, 32 devices: a whole 2x2x4 slice. The times are simulated.
32 devices in a mesh: rep: 2 (over y), enc: 4 (over z), ans: 2 (over x), sub: 2 (over core).
Axes of the slice: x: 2, y: 2, z: 4, core: 2. Of those that a mesh axis runs over, the one named last changes fastest.
Arguments:
- queries: bfloat16 [4, 4, 256, 4096], P(('rep', 'ans'), 'enc', None, 'sub'), parts along dimension 0, may hold values from -10 to 10
- own_keys: bfloat16 [4, 4, 256, 1024], P(('rep', 'ans'), 'enc', None, 'sub'), parts along dimension 0, may hold values from -6 to 6
- own_values: bfloat16 [4, 4, 256, 1024], P(('rep', 'ans'), 'enc', None, 'sub'), parts along dimension 0, may hold values from -6 to 6
- grad_out: bfloat16 [4, 4, 256, 4096], P(('rep', 'ans'), 'enc', None, 'sub'), parts along dimension 0, may hold values from -6 to 6
- passage_keys: bfloat16 [4, 32, 24, 1024], P(('rep', 'ans'), 'enc', None, 'sub'), parts along dimension 0, may hold values from -10 to 10
- passage_values: bfloat16 [4, 32, 24, 1024], P(('rep', 'ans'), 'enc', None, 'sub'), parts along dimension 0, may hold values from -6 to 6
- citations: int32 [4, 4, 6], P(('rep', 'ans'), 'enc'), parts along dimension 0, may hold values from 0 to 31, as said below
- lengths: int32 [4, 4], P(('rep', 'ans'), 'enc'), parts along dimension 0, may hold values from 64 to 256
Outputs:
- grad_queries: bfloat16 [4, 4, 256, 4096], P(('rep', 'ans'), 'enc', None, 'sub'), parts along dimension 0
- grad_own_keys: bfloat16 [4, 4, 256, 1024], P(('rep', 'ans'), 'enc', None, 'sub'), parts along dimension 0
- grad_own_values: bfloat16 [4, 4, 256, 1024], P(('rep', 'ans'), 'enc', None, 'sub'), parts along dimension 0
- grad_passage_keys: bfloat16 [4, 32, 24, 1024], P(('rep', 'ans'), 'enc', None, 'sub'), parts along dimension 0
- grad_passage_values: bfloat16 [4, 32, 24, 1024], P(('rep', 'ans'), 'enc', None, 'sub'), parts along dimension 0
There are 2 independent parts, one for each index of `rep`. A program takes and returns all parts, laid end to end along the dimension named above; each array names one. Nothing has to cross between parts.
Inputs may be any that keep to these rules, and one draw needn't show every extreme that they name: `citations`: each request cites 6 different passages of its own group. Passage p is held by index p // 8 of enc. The requests of one index of enc cite together at most 2 different passages of any one holder, and one request of each index of enc cites 2 passages of one holder.
All inputs are finite; a program needn't handle non-finite values.
Results may differ from a plain program's by a relative error of at most 0.012.
The roundings to bfloat16 on the way count: a program that leaves them out, or rounds other values in their place, can miss the bound.
Values may be sent and summed in bfloat16 or wider, within the bound.
A program may use at most 64 MiB of HBM per device.

v0:
```python
import math

import jax
import jax.numpy as jnp
from jax import lax
from jax.sharding import PartitionSpec as P

HEAD_DIM = 128
CAP = 2


THETA = 500000.0


def rotate(values, positions, direction):
    dims_shape = values.shape
    head_count = dims_shape[-1] // HEAD_DIM
    half_dim = HEAD_DIM // 2
    split_parts = values.reshape(dims_shape[:-1] + (head_count, 2, half_dim))
    inv_freq = THETA ** (-2.0 * jnp.arange(half_dim, dtype=jnp.float32) / HEAD_DIM)
    angles = positions.astype(jnp.float32)[:, None] * inv_freq[None, :]
    cosine = jnp.cos(angles)[:, None, :]
    sine_part = direction * jnp.sin(angles)[:, None, :]
    first_half = split_parts[..., 0, :]
    second_half = split_parts[..., 1, :]
    turned = jnp.stack(
        [
            first_half * cosine - second_half * sine_part,
            second_half * cosine + first_half * sine_part,
        ],
        axis=-2,
    )
    return turned.reshape(dims_shape)


def product(form, left, right):
    return jnp.einsum(form, left, right, preferred_element_type=jnp.float32)


def backward_one(
    query_rows, own_key_rows, own_value_rows, grad_rows, cited_keys, cited_values, length_value
):
    query_count, feature_count = query_rows.shape
    cite_count, passage_len, key_features = cited_keys.shape
    kv_count = key_features // HEAD_DIM
    group_size = feature_count // key_features
    prefix = cite_count * passage_len
    key_count = prefix + query_count
    query_pos = prefix + jnp.arange(query_count, dtype=jnp.int32)
    key_pos = jnp.arange(key_count, dtype=jnp.int32)
    rot_queries = rotate(query_rows.astype(jnp.float32), query_pos, 1.0).astype(jnp.bfloat16)
    all_keys = jnp.concatenate([cited_keys.reshape(prefix, key_features), own_key_rows], axis=0)
    rot_keys = rotate(all_keys.astype(jnp.float32), key_pos, 1.0).astype(jnp.bfloat16)
    all_values = jnp.concatenate(
        [cited_values.reshape(prefix, key_features), own_value_rows], axis=0
    )
    live_rows = jnp.arange(query_count, dtype=jnp.int32) < length_value
    live_grad = jnp.where(live_rows[:, None], grad_rows, jnp.zeros_like(grad_rows))
    query_heads = jnp.moveaxis(
        rot_queries.reshape(query_count, kv_count, group_size, HEAD_DIM), 1, 0
    )
    grad_heads = jnp.moveaxis(live_grad.reshape(query_count, kv_count, group_size, HEAD_DIM), 1, 0)
    key_heads = jnp.moveaxis(rot_keys.reshape(key_count, kv_count, HEAD_DIM), 1, 0)
    value_heads = jnp.moveaxis(all_values.reshape(key_count, kv_count, HEAD_DIM), 1, 0)
    score_scale = 1.0 / math.sqrt(HEAD_DIM)
    allowed = (key_pos[None, :] < prefix) | (
        key_pos[None, :] - prefix <= jnp.arange(query_count, dtype=jnp.int32)[:, None]
    )

    def head_core(head_item):
        query_one, grad_one, key_one, value_one = head_item
        scores = product("qgd,kd->gqk", query_one, key_one) * score_scale
        scores = jnp.where(allowed, scores, -1e30)
        highest = jnp.max(scores, axis=-1, keepdims=True)
        weights = jnp.exp(scores - highest)
        weights = weights / jnp.sum(weights, axis=-1, keepdims=True)
        weights_low = weights.astype(jnp.bfloat16)
        grad_values = product("gqk,qgd->kd", weights_low, grad_one)
        grad_weights = product("qgd,kd->gqk", grad_one, value_one)
        center = jnp.sum(grad_weights * weights, axis=-1, keepdims=True)
        grad_scores = (weights * (grad_weights - center) * score_scale).astype(jnp.bfloat16)
        grad_query_one = product("gqk,kd->qgd", grad_scores, key_one)
        grad_key_one = product("gqk,qgd->kd", grad_scores, query_one)
        return (grad_values, grad_query_one, grad_key_one)

    value_stack, query_stack, key_stack = lax.map(
        head_core, (query_heads, grad_heads, key_heads, value_heads)
    )
    grad_values = jnp.moveaxis(value_stack, 0, 1).reshape(key_count, key_features)
    grad_rot_queries = jnp.moveaxis(query_stack, 0, 1).reshape(query_count, feature_count)
    grad_rot_keys = jnp.moveaxis(key_stack, 0, 1).reshape(key_count, key_features)
    query_grads = rotate(grad_rot_queries, query_pos, -1.0).astype(jnp.bfloat16)
    key_grads = rotate(grad_rot_keys, key_pos, -1.0)
    value_low = grad_values.astype(jnp.bfloat16)
    key_low = key_grads.astype(jnp.bfloat16)
    return (
        query_grads,
        key_low[prefix:],
        value_low[prefix:],
        key_low[:prefix].reshape(cite_count, passage_len, key_features),
        value_low[:prefix].reshape(cite_count, passage_len, key_features),
    )


def shards(
    queries, own_keys, own_values, grad_out, passage_keys, passage_values, citations, lengths
):
    peer_count = lax.axis_size("enc")
    request_count = citations.shape[1]
    cite_count = citations.shape[2]
    held_count = passage_keys.shape[1]
    passage_len = passage_keys.shape[2]
    key_features = passage_keys.shape[3]
    cited_ids = citations[0]
    owner_ids = cited_ids // held_count
    row_ids = cited_ids % held_count
    order_cite = jnp.arange(cite_count, dtype=jnp.int32)
    earlier = order_cite[None, :] < order_cite[:, None]
    same_owner = owner_ids[:, :, None] == owner_ids[:, None, :]
    rank_ids = jnp.sum((same_owner & earlier[None, :, :]).astype(jnp.int32), axis=2)
    slot_width = request_count * CAP
    slot_ids = (
        owner_ids * request_count + jnp.arange(request_count, dtype=jnp.int32)[:, None]
    ) * CAP + rank_ids
    flat_slots = slot_ids.reshape(-1)
    wanted = (
        jnp.zeros((peer_count * slot_width,), jnp.int32).at[flat_slots].set(row_ids.reshape(-1))
    )
    wanted = wanted.reshape(peer_count, slot_width)
    asked_rows = lax.all_to_all(wanted, "enc", split_axis=0, concat_axis=0, tiled=True)
    sent_keys = passage_keys[0][asked_rows]
    sent_values = passage_values[0][asked_rows]
    came_keys = lax.all_to_all(sent_keys, "enc", split_axis=0, concat_axis=0, tiled=True)
    came_values = lax.all_to_all(sent_values, "enc", split_axis=0, concat_axis=0, tiled=True)
    slot_keys = came_keys.reshape(peer_count * slot_width, passage_len, key_features)
    slot_values = came_values.reshape(peer_count * slot_width, passage_len, key_features)

    def run_request(request_item):
        query_rows, key_rows, value_rows, grad_rows, slot_row, length_value = request_item
        return backward_one(
            query_rows,
            key_rows,
            value_rows,
            grad_rows,
            slot_keys[slot_row],
            slot_values[slot_row],
            length_value,
        )

    query_grads, own_key_grads, own_value_grads, cite_key_grads, cite_value_grads = lax.map(
        run_request, (queries[0], own_keys[0], own_values[0], grad_out[0], slot_ids, lengths[0])
    )
    flat_keys = cite_key_grads.reshape(-1, passage_len, key_features)
    flat_values = cite_value_grads.reshape(-1, passage_len, key_features)
    slot_shape = (peer_count, slot_width, passage_len, key_features)
    buffer_shape = (peer_count * slot_width, passage_len, key_features)
    send_keys = jnp.zeros(buffer_shape, jnp.bfloat16).at[flat_slots].set(flat_keys)
    send_values = jnp.zeros(buffer_shape, jnp.bfloat16).at[flat_slots].set(flat_values)
    back_keys, back_values = (
        lax.all_to_all(
            send_keys.reshape(slot_shape), "enc", split_axis=0, concat_axis=0, tiled=True
        ),
        lax.all_to_all(
            send_values.reshape(slot_shape), "enc", split_axis=0, concat_axis=0, tiled=True
        ),
    )
    rows_back = asked_rows.reshape(-1)
    total_keys = (
        jnp.zeros((held_count, passage_len, key_features), jnp.float32)
        .at[rows_back]
        .add(back_keys.reshape(buffer_shape).astype(jnp.float32))
    )
    total_values = (
        jnp.zeros((held_count, passage_len, key_features), jnp.float32)
        .at[rows_back]
        .add(back_values.reshape(buffer_shape).astype(jnp.float32))
    )
    return (
        query_grads[None],
        own_key_grads[None],
        own_value_grads[None],
        total_keys.astype(jnp.bfloat16)[None],
        total_values.astype(jnp.bfloat16)[None],
    )


def solution(mesh):
    placed = (
        P(("rep", "ans"), "enc", None, "sub"),
        P(("rep", "ans"), "enc", None, "sub"),
        P(("rep", "ans"), "enc", None, "sub"),
        P(("rep", "ans"), "enc", None, "sub"),
        P(("rep", "ans"), "enc", None, "sub"),
        P(("rep", "ans"), "enc", None, "sub"),
        P(("rep", "ans"), "enc", None),
        P(("rep", "ans"), "enc"),
    )
    return jax.shard_map(
        shards,
        mesh=mesh,
        in_specs=placed,
        out_specs=(
            P(("rep", "ans"), "enc", None, "sub"),
            P(("rep", "ans"), "enc", None, "sub"),
            P(("rep", "ans"), "enc", None, "sub"),
            P(("rep", "ans"), "enc", None, "sub"),
            P(("rep", "ans"), "enc", None, "sub"),
        ),
        check_vma=False,
    )
```

profile of v0, /device:TPU:0, one launch (start us, length us, event | category | flops | bytes accessed | tf_op | source)
XLA Modules:
  0.0 133.1 jit_solution(9029441230180430648)
XLA Ops:
  4.2 6.3 %all-to-all-start = ((s32[4,1,2]{2,1,0:T(1,128)}), s32[4,1,2]{2,1,0:T(1,128)S(1)}, u32[]{:S(2)}, u32[]{:S(2)}) async-start(s32[4,1,2]{2,1,0:T(1,128)} %bitcast.6), calls=%async_computation | async-start | bytes 4096 | tf_op jit(solution)/shard_map/all_to_all | solution.py:130
  25.1 5.1 %all-to-all-start.1 = ((bf16[4,2,24,512]{3,2,1,0:T(8,128)(2,1)}), bf16[4,2,24,512]{3,2,1,0:T(8,128)(2,1)S(1)}, u32[]{:S(2)}, u32[]{:S(2)}) async-start(bf16[4,2,24,512]{3,2,1,0:T(8,128)(2,1)} %bitcast.8), calls=%async_computation.1 | async-start | bytes 393216 | tf_op jit(solution)/shard_map/all_to_all | solution.py:133
  32.8 4.7 %all-to-all-done.1 = bf16[4,2,24,512]{3,2,1,0:T(8,128)(2,1)S(1)} async-done(((bf16[4,2,24,512]{3,2,1,0:T(8,128)(2,1)}), bf16[4,2,24,512]{3,2,1,0:T(8,128)(2,1)S(1)}, u32[]{:S(2)}, u32[]{:S(2)}) %all-to-all-start.1) | async-done | bytes 196640 | tf_op jit(solution)/shard_map/all_to_all | solution.py:133
  37.4 3.4 %all-to-all-start.2 = ((bf16[4,2,24,512]{3,2,1,0:T(8,128)(2,1)}), bf16[4,2,24,512]{3,2,1,0:T(8,128)(2,1)S(1)}, u32[]{:S(2)}, u32[]{:S(2)}) async-start(bf16[4,2,24,512]{3,2,1,0:T(8,128)(2,1)} %bitcast.21), calls=%async_computation.2 | async-start | bytes 393216 | tf_op jit(solution)/shard_map/all_to_all | solution.py:134
  43.3 3.8 %all-to-all-done.2 = bf16[4,2,24,512]{3,2,1,0:T(8,128)(2,1)S(1)} async-done(((bf16[4,2,24,512]{3,2,1,0:T(8,128)(2,1)}), bf16[4,2,24,512]{3,2,1,0:T(8,128)(2,1)S(1)}, u32[]{:S(2)}, u32[]{:S(2)}) %all-to-all-start.2) | async-done | bytes 196640 | tf_op jit(solution)/shard_map/all_to_all | solution.py:134
  48.3 52.3 %while.28 = (s32[]{:T(128)}, bf16[4,400,128]{2,1,0:T(8,128)(2,1)}, f32[4,256,4,128]{1,3,2,0:T(8,128)}, f32[4,400,128]{2,1,0:T(8,128)}, bf16[4,400,128]{2,1,0:T(8...) while((s32[]{:T(128)}, bf16[4,400,128]{2,1,0:T(8,128)(2,1)}, ...), condition=%wide.region_6.7_spmd.clone, body=%wide.region_2.6_spmd.clone.sunk | while | flops 638775872 | bytes 19378244 | solution.py:86
  48.5 2.8 %exponential_reduce_fusion.2 = (f32[4,256]{1,0:T(4,128)S(1)}, f32[4,256,400]{1,2,0:T(8,128)}) fusion(pred[256,400]{0,1:T(8,128)(4,1)S(1)} %fusion.99, bf16[4,256,4,128]{1,3,2,0:T(8,128)(2,1)} %get-tuple-element.298, s32[]{:T(128)S(6)} %copy.87, bf16[4,400,128]{2,1,0:T(8,128)(2,1)} %get-tuple-element.297), kind=kOutput, calls=%fused_computation.20.clone.1 | convolution fusion | flops 106496400 | bytes 2110464 | tf_op jit(solution)/shard_map/while/body/eval_jaxpr/while/body/eval_jaxpr/sub | solution.py:75
  51.3 2.6 %fusion.100 = bf16[4,400,128]{2,1,0:T(8,128)(2,1)} fusion(bf16[4,400,128]{2,1,0:T(8,128)(2,1)} %get-tuple-element.283, s32[]{:T(128)S(6)} %copy.87, bf16[4,256,4,128]{1,3,2,0:T(8,128)(2,1)S(1)} %get-tuple-element.299, f32[4,256]{1,0:T(4,128)S(1)} %get-tuple-element.269, pred[256,400]{0,1:T(8,128)(4,1)S(1)} %fusion.99, ...), kind=kOutput, calls=%fused_computation.26.clone.1 | convolution fusion | flops 211764624 | bytes 940032 | tf_op jit(solution)/shard_map/while/body/eval_jaxpr/while/body/eval_jaxpr/gqk,qgd->kd/dot_general | solution.py:37
  54.3 3.6 %fusion.102 = f32[4,256,4,128]{1,3,2,0:T(8,128)} fusion(f32[4,256,4,128]{1,3,2,0:T(8,128)} %get-tuple-element.284, s32[]{:T(128)S(6)} %copy.87, f32[400,256,4]{1,0,2:T(8,128)S(1)} %fusion.101, bf16[4,400,128]{2,1,0:T(8,128)(2,1)} %get-tuple-element.297, f32[4,256,400]{1,2,0:T(8,128)} %get-tuple-element.270, f32[4,256]{1,0:T(4,128)S(1)} %get-tuple-element.269), kind=kOutput, calls=%fused_computation.22.clone.1 | convolution fusion | flops 107726224 | bytes 7189504 | tf_op jit(solution)/shard_map/while/body/eval_jaxpr/while/body/eval_jaxpr/gqk,kd->qgd/dot_general | solution.py:37
  57.9 3.4 %fusion.103 = f32[4,400,128]{2,1,0:T(8,128)} fusion(f32[4,400,128]{2,1,0:T(8,128)} %get-tuple-element.285, s32[]{:T(128)S(6)} %copy.87, f32[400,256,4]{1,0,2:T(8,128)S(1)} %fusion.101, bf16[4,256,4,128]{1,3,2,0:T(8,128)(2,1)} %get-tuple-element.298, f32[4,256,400]{1,2,0:T(8,128)} %get-tuple-element.270, f32[4,256]{1,0:T(4,128)S(1)} %get-tuple-element.269), kind=kOutput, calls=%fused_computation.24.clone.1 | convolution fusion | flops 107726224 | bytes 7029760 | tf_op jit(solution)/shard_map/while/body/eval_jaxpr/while/body/eval_jaxpr/gqk,qgd->kd/dot_general | solution.py:37
  61.5 2.8 %exponential_reduce_fusion.2 = (f32[4,256]{1,0:T(4,128)S(1)}, f32[4,256,400]{1,2,0:T(8,128)}) fusion(pred[256,400]{0,1:T(8,128)(4,1)S(1)} %fusion.99, bf16[4,256,4,128]{1,3,2,0:T(8,128)(2,1)} %get-tuple-element.298, s32[]{:T(128)S(6)} %copy.87, bf16[4,400,128]{2,1,0:T(8,128)(2,1)} %get-tuple-element.297), kind=kOutput, calls=%fused_computation.20.clone.1 | convolution fusion | flops 106496400 | bytes 2110464 | tf_op jit(solution)/shard_map/while/body/eval_jaxpr/while/body/eval_jaxpr/sub | solution.py:75
  64.4 2.6 %fusion.100 = bf16[4,400,128]{2,1,0:T(8,128)(2,1)} fusion(bf16[4,400,128]{2,1,0:T(8,128)(2,1)} %get-tuple-element.283, s32[]{:T(128)S(6)} %copy.87, bf16[4,256,4,128]{1,3,2,0:T(8,128)(2,1)S(1)} %get-tuple-element.299, f32[4,256]{1,0:T(4,128)S(1)} %get-tuple-element.269, pred[256,400]{0,1:T(8,128)(4,1)S(1)} %fusion.99, ...), kind=kOutput, calls=%fused_computation.26.clone.1 | convolution fusion | flops 211764624 | bytes 940032 | tf_op jit(solution)/shard_map/while/body/eval_jaxpr/while/body/eval_jaxpr/gqk,qgd->kd/dot_general | solution.py:37
  67.4 3.6 %fusion.102 = f32[4,256,4,128]{1,3,2,0:T(8,128)} fusion(f32[4,256,4,128]{1,3,2,0:T(8,128)} %get-tuple-element.284, s32[]{:T(128)S(6)} %copy.87, f32[400,256,4]{1,0,2:T(8,128)S(1)} %fusion.101, bf16[4,400,128]{2,1,0:T(8,128)(2,1)} %get-tuple-element.297, f32[4,256,400]{1,2,0:T(8,128)} %get-tuple-element.270, f32[4,256]{1,0:T(4,128)S(1)} %get-tuple-element.269), kind=kOutput, calls=%fused_computation.22.clone.1 | convolution fusion | flops 107726224 | bytes 7189504 | tf_op jit(solution)/shard_map/while/body/eval_jaxpr/while/body/eval_jaxpr/gqk,kd->qgd/dot_general | solution.py:37
  71.0 3.5 %fusion.103 = f32[4,400,128]{2,1,0:T(8,128)} fusion(f32[4,400,128]{2,1,0:T(8,128)} %get-tuple-element.285, s32[]{:T(128)S(6)} %copy.87, f32[400,256,4]{1,0,2:T(8,128)S(1)} %fusion.101, bf16[4,256,4,128]{1,3,2,0:T(8,128)(2,1)} %get-tuple-element.298, f32[4,256,400]{1,2,0:T(8,128)} %get-tuple-element.270, f32[4,256]{1,0:T(4,128)S(1)} %get-tuple-element.269), kind=kOutput, calls=%fused_computation.24.clone.1 | convolution fusion | flops 107726224 | bytes 7029760 | tf_op jit(solution)/shard_map/while/body/eval_jaxpr/while/body/eval_jaxpr/gqk,qgd->kd/dot_general | solution.py:37
  74.7 2.8 %exponential_reduce_fusion.2 = (f32[4,256]{1,0:T(4,128)S(1)}, f32[4,256,400]{1,2,0:T(8,128)}) fusion(pred[256,400]{0,1:T(8,128)(4,1)S(1)} %fusion.99, bf16[4,256,4,128]{1,3,2,0:T(8,128)(2,1)} %get-tuple-element.298, s32[]{:T(128)S(6)} %copy.87, bf16[4,400,128]{2,1,0:T(8,128)(2,1)} %get-tuple-element.297), kind=kOutput, calls=%fused_computation.20.clone.1 | convolution fusion | flops 106496400 | bytes 2110464 | tf_op jit(solution)/shard_map/while/body/eval_jaxpr/while/body/eval_jaxpr/sub | solution.py:75
  77.5 2.6 %fusion.100 = bf16[4,400,128]{2,1,0:T(8,128)(2,1)} fusion(bf16[4,400,128]{2,1,0:T(8,128)(2,1)} %get-tuple-element.283, s32[]{:T(128)S(6)} %copy.87, bf16[4,256,4,128]{1,3,2,0:T(8,128)(2,1)S(1)} %get-tuple-element.299, f32[4,256]{1,0:T(4,128)S(1)} %get-tuple-element.269, pred[256,400]{0,1:T(8,128)(4,1)S(1)} %fusion.99, ...), kind=kOutput, calls=%fused_computation.26.clone.1 | convolution fusion | flops 211764624 | bytes 940032 | tf_op jit(solution)/shard_map/while/body/eval_jaxpr/while/body/eval_jaxpr/gqk,qgd->kd/dot_general | solution.py:37
  80.5 3.6 %fusion.102 = f32[4,256,4,128]{1,3,2,0:T(8,128)} fusion(f32[4,256,4,128]{1,3,2,0:T(8,128)} %get-tuple-element.284, s32[]{:T(128)S(6)} %copy.87, f32[400,256,4]{1,0,2:T(8,128)S(1)} %fusion.101, bf16[4,400,128]{2,1,0:T(8,128)(2,1)} %get-tuple-element.297, f32[4,256,400]{1,2,0:T(8,128)} %get-tuple-element.270, f32[4,256]{1,0:T(4,128)S(1)} %get-tuple-element.269), kind=kOutput, calls=%fused_computation.22.clone.1 | convolution fusion | flops 107726224 | bytes 7189504 | tf_op jit(solution)/shard_map/while/body/eval_jaxpr/while/body/eval_jaxpr/gqk,kd->qgd/dot_general | solution.py:37
  84.1 3.4 %fusion.103 = f32[4,400,128]{2,1,0:T(8,128)} fusion(f32[4,400,128]{2,1,0:T(8,128)} %get-tuple-element.285, s32[]{:T(128)S(6)} %copy.87, f32[400,256,4]{1,0,2:T(8,128)S(1)} %fusion.101, bf16[4,256,4,128]{1,3,2,0:T(8,128)(2,1)} %get-tuple-element.298, f32[4,256,400]{1,2,0:T(8,128)} %get-tuple-element.270, f32[4,256]{1,0:T(4,128)S(1)} %get-tuple-element.269), kind=kOutput, calls=%fused_computation.24.clone.1 | convolution fusion | flops 107726224 | bytes 7029760 | tf_op jit(solution)/shard_map/while/body/eval_jaxpr/while/body/eval_jaxpr/gqk,qgd->kd/dot_general | solution.py:37
  87.7 2.8 %exponential_reduce_fusion.2 = (f32[4,256]{1,0:T(4,128)S(1)}, f32[4,256,400]{1,2,0:T(8,128)}) fusion(pred[256,400]{0,1:T(8,128)(4,1)S(1)} %fusion.99, bf16[4,256,4,128]{1,3,2,0:T(8,128)(2,1)} %get-tuple-element.298, s32[]{:T(128)S(6)} %copy.87, bf16[4,400,128]{2,1,0:T(8,128)(2,1)} %get-tuple-element.297), kind=kOutput, calls=%fused_computation.20.clone.1 | convolution fusion | flops 106496400 | bytes 2110464 | tf_op jit(solution)/shard_map/while/body/eval_jaxpr/while/body/eval_jaxpr/sub | solution.py:75
  93.5 3.6 %fusion.102 = f32[4,256,4,128]{1,3,2,0:T(8,128)} fusion(f32[4,256,4,128]{1,3,2,0:T(8,128)} %get-tuple-element.284, s32[]{:T(128)S(6)} %copy.87, f32[400,256,4]{1,0,2:T(8,128)S(1)} %fusion.101, bf16[4,400,128]{2,1,0:T(8,128)(2,1)} %get-tuple-element.297, f32[4,256,400]{1,2,0:T(8,128)} %get-tuple-element.270, f32[4,256]{1,0:T(4,128)S(1)} %get-tuple-element.269), kind=kOutput, calls=%fused_computation.22.clone.1 | convolution fusion | flops 107726224 | bytes 7189504 | tf_op jit(solution)/shard_map/while/body/eval_jaxpr/while/body/eval_jaxpr/gqk,kd->qgd/dot_general | solution.py:37
  97.1 3.4 %fusion.103 = f32[4,400,128]{2,1,0:T(8,128)} fusion(f32[4,400,128]{2,1,0:T(8,128)} %get-tuple-element.285, s32[]{:T(128)S(6)} %copy.87, f32[400,256,4]{1,0,2:T(8,128)S(1)} %fusion.101, bf16[4,256,4,128]{1,3,2,0:T(8,128)(2,1)} %get-tuple-element.298, f32[4,256,400]{1,2,0:T(8,128)} %get-tuple-element.270, f32[4,256]{1,0:T(4,128)S(1)} %get-tuple-element.269), kind=kOutput, calls=%fused_computation.24.clone.1 | convolution fusion | flops 107726224 | bytes 7029760 | tf_op jit(solution)/shard_map/while/body/eval_jaxpr/while/body/eval_jaxpr/gqk,qgd->kd/dot_general | solution.py:37
  107.3 4.0 %all-to-all-start.3 = ((bf16[4,2,24,512]{3,2,1,0:T(8,128)(2,1)}), bf16[4,2,24,512]{3,2,1,0:T(8,128)(2,1)}, u32[]{:S(2)}, u32[]{:S(2)}) async-start(bf16[4,2,24,512]{3,2,1,0:T(8,128)(2,1)} %bitcast.35), calls=%async_computation.3 | async-start | bytes 393216 | tf_op jit(solution)/shard_map/all_to_all | solution.py:160
  120.0 5.1 %all-to-all-start.4 = ((bf16[4,2,24,512]{3,2,1,0:T(8,128)(2,1)}), bf16[4,2,24,512]{3,2,1,0:T(8,128)(2,1)S(1)}, u32[]{:S(2)}, u32[]{:S(2)}) async-start(bf16[4,2,24,512]{3,2,1,0:T(8,128)(2,1)} %bitcast.38), calls=%async_computation.4 | async-start | bytes 393216 | tf_op jit(solution)/shard_map/all_to_all | solution.py:163
  127.8 3.6 %all-to-all-done.4 = bf16[4,2,24,512]{3,2,1,0:T(8,128)(2,1)S(1)} async-done(((bf16[4,2,24,512]{3,2,1,0:T(8,128)(2,1)}), bf16[4,2,24,512]{3,2,1,0:T(8,128)(2,1)S(1)}, u32[]{:S(2)}, u32[]{:S(2)}) %all-to-all-start.4) | async-done | bytes 196640 | tf_op jit(solution)/shard_map/all_to_all | solution.py:163
  (110 shorter events, 48.0 us)
Async XLA Ops:
  0.6 23.2 %copy-start = (bf16[1,8,24,512]{3,2,1,0:T(8,128)(2,1)S(1)}, bf16[1,8,24,512]{3,2,1,0:T(8,128)(2,1)}, u32[]{:S(2)}) copy-start(bf16[1,8,24,512]{3,2,1,0:T(8,128)(2,1)} %param.14) | copy-start | bytes 589828
  4.2 19.3 %all-to-all-start = ((s32[4,1,2]{2,1,0:T(1,128)}), s32[4,1,2]{2,1,0:T(1,128)S(1)}, u32[]{:S(2)}, u32[]{:S(2)}) async-start(s32[4,1,2]{2,1,0:T(1,128)} %bitcast.6), calls=%async_computation | async-start | bytes 4096 | tf_op jit(solution)/shard_map/all_to_all | solution.py:130
  14.1 5.7 %copy-start.8 = (bf16[1,1,256,512]{3,2,1,0:T(8,128)(2,1)S(1)}, bf16[1,1,256,512]{3,2,1,0:T(8,128)(2,1)}, u32[]{:S(2)}) copy-start(bf16[1,1,256,512]{3,2,1,0:T(8,128)(2,1)} %param.12) | copy-start | bytes 786436
  21.8 1.6 %copy-start.1 = (bf16[1,1,256,2048]{2,3,1,0:T(8,128)(2,1)S(1)}, bf16[1,1,256,2048]{2,3,1,0:T(8,128)(2,1)}, u32[]{:S(2)}) copy-start(bf16[1,1,256,2048]{2,3,1,0:T(8,128)(2,1)} %copy.65) | copy-start | bytes 3145732
  21.8 1.6 %copy-start.10 = (pred[256]{0:T(512)(128)(4,1)S(1)}, pred[256]{0:T(512)(128)(4,1)}, u32[]{:S(2)}) copy-start(pred[256]{0:T(512)(128)(4,1)} %iota_compare_fusion.2) | copy-start | bytes 772
  22.9 7.3 %copy-start.9 = (bf16[1,8,24,512]{3,2,1,0:T(8,128)(2,1)S(1)}, bf16[1,8,24,512]{3,2,1,0:T(8,128)(2,1)}, u32[]{:S(2)}) copy-start(bf16[1,8,24,512]{3,2,1,0:T(8,128)(2,1)} %param.15) | copy-start | bytes 589828
  23.5 18.3 %copy-start.4 = (bf16[1,1,256,512]{2,3,1,0:T(8,128)(2,1)S(1)}, bf16[1,1,256,512]{2,3,1,0:T(8,128)(2,1)}, u32[]{:S(2)}) copy-start(bf16[1,1,256,512]{2,3,1,0:T(8,128)(2,1)} %copy.62) | copy-start | bytes 786436
  25.1 12.4 %all-to-all-start.1 = ((bf16[4,2,24,512]{3,2,1,0:T(8,128)(2,1)}), bf16[4,2,24,512]{3,2,1,0:T(8,128)(2,1)S(1)}, u32[]{:S(2)}, u32[]{:S(2)}) async-start(bf16[4,2,24,512]{3,2,1,0:T(8,128)(2,1)} %bitcast.8), calls=%async_computation.1 | async-start | bytes 393216 | tf_op jit(solution)/shard_map/all_to_all | solution.py:133
  32.7 9.3 %copy-start.6 = (f32[400,64]{0,1:T(8,128)S(1)}, f32[400,64]{0,1:T(8,128)}, u32[]{:S(2)}) copy-start(f32[400,64]{0,1:T(8,128)} %get-tuple-element.199) | copy-start | bytes 307204
  37.4 9.6 %all-to-all-start.2 = ((bf16[4,2,24,512]{3,2,1,0:T(8,128)(2,1)}), bf16[4,2,24,512]{3,2,1,0:T(8,128)(2,1)S(1)}, u32[]{:S(2)}, u32[]{:S(2)}) async-start(bf16[4,2,24,512]{3,2,1,0:T(8,128)(2,1)} %bitcast.21), calls=%async_computation.2 | async-start | bytes 393216 | tf_op jit(solution)/shard_map/all_to_all | solution.py:134
  42.2 5.6 %copy-start.3 = (bf16[1,1,256,512]{2,3,1,0:T(8,128)(2,1)S(1)}, bf16[1,1,256,512]{2,3,1,0:T(8,128)(2,1)}, u32[]{:S(2)}) copy-start(bf16[1,1,256,512]{2,3,1,0:T(8,128)(2,1)} %copy.66) | copy-start | bytes 786436
  100.6 1.5 %copy-start.5 = (f32[400,64]{0,1:T(8,128)S(1)}, f32[400,64]{0,1:T(8,128)}, u32[]{:S(2)}) copy-start(f32[400,64]{0,1:T(8,128)} %get-tuple-element.198) | copy-start | bytes 307204
  102.3 9.0 %copy-start.2 = (f32[4,256,4,128]{1,3,2,0:T(8,128)S(1)}, f32[4,256,4,128]{1,3,2,0:T(8,128)}, u32[]{:S(2)}) copy-start(f32[4,256,4,128]{1,3,2,0:T(8,128)} %get-tuple-element.96) | copy-start | bytes 6291460
  102.3 9.0 %copy-start.7 = (f32[256,64]{0,1:T(8,128)S(1)}, f32[256,64]{0,1:T(8,128)}, u32[]{:S(2)}) copy-start(f32[256,64]{0,1:T(8,128)} %get-tuple-element.201) | copy-start | bytes 196612
  107.3 12.7 %all-to-all-start.3 = ((bf16[4,2,24,512]{3,2,1,0:T(8,128)(2,1)}), bf16[4,2,24,512]{3,2,1,0:T(8,128)(2,1)}, u32[]{:S(2)}, u32[]{:S(2)}) async-start(bf16[4,2,24,512]{3,2,1,0:T(8,128)(2,1)} %bitcast.35), calls=%async_computation.3 | async-start | bytes 393216 | tf_op jit(solution)/shard_map/all_to_all | solution.py:160
  120.0 11.3 %all-to-all-start.4 = ((bf16[4,2,24,512]{3,2,1,0:T(8,128)(2,1)}), bf16[4,2,24,512]{3,2,1,0:T(8,128)(2,1)S(1)}, u32[]{:S(2)}, u32[]{:S(2)}) async-start(bf16[4,2,24,512]{3,2,1,0:T(8,128)(2,1)} %bitcast.38), calls=%async_computation.4 | async-start | bytes 393216 | tf_op jit(solution)/shard_map/all_to_all | solution.py:163
where the time goes:
time: 134 us; the launch traced here: 133 us
  matrix products  51.5 us (38%)
  local copies, waits for them, and re-layouts  28.4 us (21%)
  starting transfers between devices  23.8 us (18%)
  other arithmetic  15.6 us (12%)
  waiting for transfers between devices  12 us (9%)
  between operations  1.7 us (1%)
    dot_general x16, matrix products, product(): return jnp.einsum(form, left, right, preferred_element_type=jnp.float32)  40.3 us
    sub x4, matrix products, head_core(): weights = jnp.exp(scores - highest)  11.3 us
    unnamed x30, local copies, waits for them, and re-layouts  10.4 us
    all_to_all x1, starting transfers between devices, shards(): lax.all_to_all(wanted, 'enc', split_axis=0, concat_axis=0, tiled=True)  6.32 us
    all_to_all x1, starting transfers between devices, shards(): lax.all_to_all(sent_keys, 'enc', split_axis=0, concat_axis=0, tiled=True)  5.09 us
    all_to_all x1, starting transfers between devices, shards(): lax.all_to_all(send_values.reshape(slot_shape), 'enc', split_axis=0, conc...  5.05 us
    all_to_all x1, waiting for transfers between devices, shards(): lax.all_to_all(sent_keys, 'enc', split_axis=0, concat_axis=0, tiled=True)  4.66 us
    all_to_all x1, starting transfers between devices, shards(): lax.all_to_all(send_keys.reshape(slot_shape), 'enc', split_axis=0, concat...  4 us
  transfers between devices with their start and end apart: 5, of which 3 were waited for; matrix products, arithmetic and copies ran while one was open for 21% of the time, Pallas kernels for 0%

commit v1 on v0

v1 whole, which is shorter than its diff:
```python
import functools
import math

import jax
import jax.numpy as jnp
import numpy as np
from jax import lax
from jax.experimental import pallas as pl
from jax.experimental.pallas import tpu as pltpu
from jax.sharding import PartitionSpec as P

D = 128
CAP = 2
THETA = 500000.0
SCALE = 1.0 / math.sqrt(D)
MESH = pl.DeviceIdType.MESH
F32 = jnp.float32
BF16 = jnp.bfloat16


def tables(count):
    half = D // 2
    inv = np.float32(THETA) ** (np.float32(-2.0) * np.arange(half, dtype=np.float32) / np.float32(D))
    angles = np.arange(count, dtype=np.float32)[:, None] * inv.astype(np.float32)[None, :]
    cos, sin = np.cos(angles), np.sin(angles)
    return np.concatenate([cos, cos, -sin, sin], axis=1).astype(np.float32)


def turn(x, table, sign):
    cos, sin = table[:, :D], table[:, D:]
    return x * cos + sign * (pltpu.roll(x, D // 2, 1) * sin)


def dot_nt(a, b):
    return lax.dot_general(a, b, (((1,), (1,)), ((), ())), preferred_element_type=F32)


def dot_nn(a, b):
    return lax.dot_general(a, b, (((1,), (0,)), ((), ())), preferred_element_type=F32)


def dot_tn(a, b):
    return lax.dot_general(a, b, (((0,), (0,)), ((), ())), preferred_element_type=F32)


def kernel(
    n, cites, lens, q_hbm, ok_hbm, ov_hbm, go_hbm, pk_hbm, pv_hbm, tab_hbm,
    gq, gok, gov, gpk, gpv,
    q, ok, ov, go, pk, pv, tab,
    tile, tiles_in, sendbuf, fwd_in, backbuf, back_in,
    stage, gstage, qr, gl, ko, kp, dsp, es, dps, stats, wrow, slot_of, cite_of,
    load_sem, cs_sem, cr_sem, fs_sem, fr_sem, bs_sem, br_sem,
):
    rows = q.shape[0]
    heads = ok.shape[1] // D
    group = q.shape[1] // ok.shape[1]
    held, plen = pk.shape[0], pk.shape[1]
    ncite = cites.shape[2]
    prefix = ncite * plen
    me = lax.axis_index("enc")

    loads = [
        pltpu.make_async_copy(src, dst, load_sem.at[i])
        for i, (src, dst) in enumerate(
            [
                (pk_hbm.at[0], pk), (pv_hbm.at[0], pv), (tab_hbm, tab),
                (ok_hbm.at[0, 0], ok), (ov_hbm.at[0, 0], ov),
                (q_hbm.at[0, 0], q), (go_hbm.at[0, 0], go),
            ]
        )
    ]
    barrier = pltpu.get_barrier_semaphore()

    @pl.loop(1, n)
    def _(k):
        pl.semaphore_signal(
            barrier, inc=1, device_id={"enc": lax.rem(me + k, n)}, device_id_type=MESH
        )

    for load in loads:
        load.start()

    lane = lax.broadcasted_iota(jnp.int32, (8, D), 1)
    wanted = jnp.full((8, D), -1, jnp.int32)
    for j in range(ncite):
        wanted = jnp.where(lane == j, cites[0, 0, j], wanted)
    tile[...] = wanted
    tiles_in[0] = wanted
    pl.semaphore_wait(barrier, n - 1)

    def ask(k):
        return pltpu.make_async_remote_copy(
            src_ref=tile, dst_ref=tiles_in.at[k],
            send_sem=cs_sem.at[k], recv_sem=cr_sem.at[k],
            device_id={"enc": lax.rem(me + k, n)}, device_id_type=MESH,
        )

    def forward(k, h):
        return pltpu.make_async_remote_copy(
            src_ref=sendbuf.at[k, h], dst_ref=fwd_in.at[k, h],
            send_sem=fs_sem.at[k, h], recv_sem=fr_sem.at[k, h],
            device_id={"enc": lax.rem(me - k + n, n)}, device_id_type=MESH,
        )

    def back(k, h):
        return pltpu.make_async_remote_copy(
            src_ref=backbuf.at[k, h], dst_ref=back_in.at[k, h],
            send_sem=bs_sem.at[k, h], recv_sem=br_sem.at[k, h],
            device_id={"enc": lax.rem(me + k, n)}, device_id_type=MESH,
        )

    @pl.loop(1, n)
    def _(k):
        ask(k).start()

    @pl.loop(0, ncite)
    def _(j):
        mine = cites[0, 0, j]
        owner = lax.div(mine, held)

        def count(i, total):
            other = cites[0, 0, i]
            return total + jnp.where((lax.div(other, held) == owner) & (other < mine), 1, 0)

        rank = lax.fori_loop(0, ncite, count, jnp.int32(0))
        slot_of[j] = lax.rem(owner - me + n, n) * CAP + rank

    @pl.loop(0, n * CAP)
    def _(s):
        def find(j, found):
            return jnp.where(slot_of[j] == s, j, found)

        cite_of[s] = lax.fori_loop(0, ncite, find, jnp.int32(ncite))

    loads[0].wait()
    loads[1].wait()

    def pick(k, target):
        own = tiles_in[k] - me * held
        inside = (own >= 0) & (own < held) & (lane < ncite)
        low = jnp.min(jnp.where(inside, own, held))
        high = jnp.max(jnp.where(inside, own, -1))
        wrow[k, 0] = low
        wrow[k, 1] = jnp.where(high > low, high, held)
        a = jnp.clip(low, 0, held - 1)
        b = jnp.clip(high, 0, held - 1)
        block = jnp.concatenate(
            [pk[a].astype(F32), pk[b].astype(F32), pv[a].astype(F32), pv[b].astype(F32)], axis=0
        ).astype(BF16)
        for h in range(heads):
            target[k, h] = block[:, h * D : (h + 1) * D]

    @pl.loop(1, n)
    def _(k):
        ask(k).wait_recv()
        pick(k, sendbuf)

    @pl.loop(0, heads)
    def _(h):
        @pl.loop(1, n)
        def _(k):
            forward(k, h).start()

    pick(0, fwd_in)
    for load in loads[2:]:
        load.wait()

    limit = lens[0, 0]
    live = lax.broadcasted_iota(jnp.int32, (rows, D), 0) < limit
    causal = lax.broadcasted_iota(jnp.int32, (rows, rows), 0) <= lax.broadcasted_iota(
        jnp.int32, (rows, rows), 1
    )

    @pl.loop(0, heads)
    def _(h):
        own_table = tab[prefix:, :]
        kcols = pl.ds(pl.multiple_of(h * D, D), D)
        key_own = turn(ok[:, kcols].astype(F32), own_table, 1.0).astype(BF16)
        ko[h] = key_own
        value_own = ov[:, kcols]
        for j in range(group):
            cols = pl.ds(pl.multiple_of((h * group + j) * D, D), D)
            query = turn(q[:, cols].astype(F32), own_table, 1.0).astype(BF16)
            grad = jnp.where(live, go[:, cols].astype(F32), 0.0).astype(BF16)
            qr[h, j] = query
            gl[h, j] = grad
            scores = jnp.where(causal, dot_nt(key_own, query) * SCALE, -1e30)
            top = jnp.max(scores, axis=0, keepdims=True)
            weights = jnp.exp(scores - top)
            gw = dot_nt(value_own, grad)
            es[h, j] = weights
            dps[h, j] = gw
            stats[h, j, 0:1, :] = top
            stats[h, j, 1:2, :] = jnp.sum(weights, axis=0, keepdims=True)
            stats[h, j, 2:3, :] = jnp.sum(weights * gw, axis=0, keepdims=True)

    gstage[ncite] = jnp.zeros(gstage.shape[1:], F32)

    @pl.loop(0, heads)
    def _(h):
        @pl.loop(1, n)
        def _(k):
            forward(k, h).wait_recv()

        @pl.loop(0, n)
        def _(k):
            block = fwd_in[k, h].astype(F32)
            for r in range(CAP):
                stage[k * CAP + r, 0] = block[r * plen : (r + 1) * plen]
                stage[k * CAP + r, 1] = block[(CAP + r) * plen : (CAP + r + 1) * plen]

        keys = jnp.concatenate([stage[slot_of[j], 0] for j in range(ncite)], axis=0)
        key_pas = turn(keys, tab[:prefix, :], 1.0).astype(BF16)
        kp[h] = key_pas
        value_pas = jnp.concatenate(
            [stage[slot_of[j], 1] for j in range(ncite)], axis=0
        ).astype(BF16)
        sum_keys = jnp.zeros((prefix, D), F32)
        sum_values = jnp.zeros((prefix, D), F32)
        for j in range(group):
            query, grad = qr[h, j], gl[h, j]
            top = stats[h, j, 0:1, :]
            scores = dot_nt(key_pas, query) * SCALE
            highest = jnp.maximum(top, jnp.max(scores, axis=0, keepdims=True))
            weights = jnp.exp(scores - highest)
            alpha = jnp.exp(top - highest)
            total = stats[h, j, 1:2, :] * alpha + jnp.sum(weights, axis=0, keepdims=True)
            inverse = 1.0 / total
            gw = dot_nt(value_pas, grad)
            center = (
                stats[h, j, 2:3, :] * alpha + jnp.sum(weights * gw, axis=0, keepdims=True)
            ) * inverse
            weights = weights * inverse
            grad_scores = (weights * (gw - center) * SCALE).astype(BF16)
            dsp[h, j] = grad_scores
            sum_values += dot_nn(weights.astype(BF16), grad)
            sum_keys += dot_nn(grad_scores, query)
            stats[h, j, 3:4, :] = alpha * inverse
            stats[h, j, 4:5, :] = center
        sum_keys = turn(sum_keys, tab[:prefix, :], -1.0)
        for j in range(ncite):
            gstage[j, 0] = sum_keys[j * plen : (j + 1) * plen]
            gstage[j, 1] = sum_values[j * plen : (j + 1) * plen]

        def give(k, target):
            a, b = cite_of[k * CAP], cite_of[k * CAP + 1]
            target[k, h] = jnp.concatenate(
                [gstage[a, 0], gstage[b, 0], gstage[a, 1], gstage[b, 1]], axis=0
            ).astype(BF16)

        @pl.loop(1, n)
        def _(k):
            give(k, backbuf)
            back(k, h).start()

        give(0, back_in)

        kcols = pl.ds(pl.multiple_of(h * D, D), D)
        key_own = ko[h]
        own_table = tab[prefix:, :]
        own_keys = jnp.zeros((rows, D), F32)
        own_values = jnp.zeros((rows, D), F32)
        for j in range(group):
            query, grad = qr[h, j], gl[h, j]
            weights = es[h, j] * stats[h, j, 3:4, :]
            grad_scores = (weights * (dps[h, j] - stats[h, j, 4:5, :]) * SCALE).astype(BF16)
            own_values += dot_nn(weights.astype(BF16), grad)
            own_keys += dot_nn(grad_scores, query)
            grad_query = dot_tn(dsp[h, j], key_pas) + dot_tn(grad_scores, key_own)
            cols = pl.ds(pl.multiple_of((h * group + j) * D, D), D)
            gq[0, 0, :, cols] = turn(grad_query, own_table, -1.0).astype(BF16)
        gok[0, 0, :, kcols] = turn(own_keys, own_table, -1.0).astype(BF16)
        gov[0, 0, :, kcols] = own_values.astype(BF16)

    for h in range(heads):
        @pl.loop(1, n)
        def _(k):
            back(k, h).wait_recv()

        @pl.loop(0, held)
        def _(i):
            def add(k, total):
                block = back_in[k, h].astype(F32)
                for r in range(CAP):
                    hit = wrow[k, r] == i
                    total = (
                        total[0] + jnp.where(hit, block[r * plen : (r + 1) * plen], 0.0),
                        total[1]
                        + jnp.where(hit, block[(CAP + r) * plen : (CAP + r + 1) * plen], 0.0),
                    )
                return total

            zero = jnp.zeros((plen, D), F32)
            total = lax.fori_loop(0, n, add, (zero, zero))
            gpk[0, i, :, h * D : (h + 1) * D] = total[0].astype(BF16)
            gpv[0, i, :, h * D : (h + 1) * D] = total[1].astype(BF16)

    @pl.loop(1, n)
    def _(k):
        ask(k).wait_send()

        @pl.loop(0, heads)
        def _(h):
            forward(k, h).wait_send()
            back(k, h).wait_send()


def shards(n, queries, own_keys, own_values, grad_out, pkeys, pvalues, citations, lengths):
    rows, features = queries.shape[2:]
    kfeatures = own_keys.shape[3]
    heads, group = kfeatures // D, features // kfeatures
    held, plen = pkeys.shape[1], pkeys.shape[2]
    ncite = citations.shape[2]
    prefix = ncite * plen
    keys = prefix + rows
    slab = (n, heads, 2 * CAP * plen, D)
    table = jnp.asarray(tables(keys))
    any_spec = pl.BlockSpec(memory_space=pl.ANY)
    smem = pl.BlockSpec(memory_space=pltpu.SMEM)
    vmem = pl.BlockSpec(memory_space=pltpu.VMEM)
    like = lambda x: jax.ShapeDtypeStruct(x.shape, x.dtype)
    flops = 2 * 5 * heads * group * rows * keys * D
    return pl.pallas_call(
        functools.partial(kernel, n),
        out_shape=tuple(like(x) for x in (queries, own_keys, own_values, pkeys, pvalues)),
        in_specs=[smem] * 2 + [any_spec] * 7,
        out_specs=(vmem,) * 5,
        scratch_shapes=[
            pltpu.VMEM((rows, features), BF16),
            pltpu.VMEM((rows, kfeatures), BF16),
            pltpu.VMEM((rows, kfeatures), BF16),
            pltpu.VMEM((rows, features), BF16),
            pltpu.VMEM((held, plen, kfeatures), BF16),
            pltpu.VMEM((held, plen, kfeatures), BF16),
            pltpu.VMEM((keys, 2 * D), F32),
            pltpu.VMEM((8, D), jnp.int32),
            pltpu.VMEM((n, 8, D), jnp.int32),
            pltpu.VMEM(slab, BF16),
            pltpu.VMEM(slab, BF16),
            pltpu.VMEM(slab, BF16),
            pltpu.VMEM(slab, BF16),
            pltpu.VMEM((n * CAP, 2, plen, D), F32),
            pltpu.VMEM((ncite + 1, 2, plen, D), F32),
            pltpu.VMEM((heads, group, rows, D), BF16),
            pltpu.VMEM((heads, group, rows, D), BF16),
            pltpu.VMEM((heads, rows, D), BF16),
            pltpu.VMEM((heads, prefix, D), BF16),
            pltpu.VMEM((heads, group, prefix, rows), BF16),
            pltpu.VMEM((heads, group, rows, rows), F32),
            pltpu.VMEM((heads, group, rows, rows), F32),
            pltpu.VMEM((heads, group, 8, rows), F32),
            pltpu.SMEM((n, CAP), jnp.int32),
            pltpu.SMEM((ncite,), jnp.int32),
            pltpu.SMEM((n * CAP,), jnp.int32),
            pltpu.SemaphoreType.DMA((7,)),
            pltpu.SemaphoreType.DMA((n,)),
            pltpu.SemaphoreType.DMA((n,)),
            pltpu.SemaphoreType.DMA((n, heads)),
            pltpu.SemaphoreType.DMA((n, heads)),
            pltpu.SemaphoreType.DMA((n, heads)),
            pltpu.SemaphoreType.DMA((n, heads)),
        ],
        compiler_params=pltpu.CompilerParams(
            collective_id=0, has_side_effects=True, vmem_limit_bytes=56 * 1024 * 1024
        ),
        cost_estimate=pl.CostEstimate(
            flops=flops, bytes_accessed=6 * 1024 * 1024, transcendentals=heads * group * rows * keys
        ),
    )(citations, lengths, queries, own_keys, own_values, grad_out, pkeys, pvalues, table)


def solution(mesh):
    rows = P(("rep", "ans"), "enc", None, "sub")
    return jax.shard_map(
        functools.partial(shards, mesh.shape["enc"]),
        mesh=mesh,
        in_specs=(rows,) * 6 + (P(("rep", "ans"), "enc", None), P(("rep", "ans"), "enc")),
        out_specs=(rows,) * 5,
        check_vma=False,
    )
```

time: 134 us -> 37.5 us (0.28)
  matrix products: 51.5 us -> 0 us
  Pallas kernels: 0 us -> 29.9 us
  starting transfers between devices: 23.8 us -> 0 us
  local copies, waits for them, and re-layouts: 28.4 us -> 6.09 us
  other arithmetic: 15.6 us -> 0 us
  waiting for transfers between devices: 12 us -> 0 us
    dot_general x16 -> x0, matrix products: 40.3 us -> none  [product(): return jnp.einsum(form, left, right, preferred_element_type=jnp.float32)]
    pallas_call x0 -> x1, Pallas kernels: none -> 29.9 us  [shards(): pl.pallas_call(functools.partial(kernel, n), out_shape=tuple((like(x) for...]
    all_to_all x5 -> x0, starting transfers between devices: 23.8 us -> none  [the longest x1 6.32 us: shards(): lax.all_to_all(wanted, 'enc', split_axis=0, concat_axis=0, tiled=True)]
    all_to_all x5 -> x0, waiting for transfers between devices: 12 us -> none  [the longest x1 4.66 us: shards(): lax.all_to_all(sent_keys, 'enc', split_axis=0, concat_axis=0, tiled=True)]
    sub x4 -> x0, matrix products: 11.3 us -> none  [head_core(): weights = jnp.exp(scores - highest)]
    scatter x3 -> x0, local copies, waits for them, and re-layouts: 4.83 us -> none  [the longest x1 2.13 us: shards(): jnp.zeros(buffer_shape, jnp.bfloat16).at[flat_slots].set(flat_values)]
    unnamed x30 -> x13, local copies, waits for them, and re-layouts: 10.4 us -> 6.09 us
    another operation x12 -> x0, other arithmetic: 3.9 us -> none  [the longest x5 2.09 us: rotate(): jnp.stack([first_half * cosine - second_half * sine_part, second_half * c...]
  transfers between devices with their start and end apart: 5 -> 0, of which waited for: 3 -> 0; matrix products, arithmetic and copies ran while one was open for 21% -> 0% of each run, Pallas kernels for 0% -> 0%
where the time goes in v1:
time: 37.5 us; the launch traced here: 37.3 us
  Pallas kernels  29.9 us (80%)
  local copies, waits for them, and re-layouts  6.09 us (16%)
  between operations  1.3 us (3%)
    pallas_call x1, Pallas kernels, shards(): pl.pallas_call(functools.partial(kernel, n), out_shape=tuple((like(x) for...  29.9 us
    unnamed x13, local copies, waits for them, and re-layouts  6.09 us

profile of v1, /device:TPU:0, one launch (start us, length us, event | category | flops | bytes accessed | tf_op | source)
XLA Modules:
  0.0 37.3 jit_solution(6012164194069340782)
XLA Ops:
  1.3 29.9 %shard_map.128 = (bf16[1,1,256,2048]{3,2,1,0:T(8,128)(2,1)}, bf16[1,1,256,512]{3,2,1,0:T(8,128)(2,1)}, bf16[1,1,256,512]{3,2,1,0:T(8,128)(2,1)}, bf16[1,8,24,512]{3,2,1,0:T(8,128)(2,1)}, bf16[1,8,24,512]{3,2,1,0:T(8,128)(2,1)}) custom-call(s32[1,1,6]{2,1,0:T(1,128)} %cites.1, s32[1,1]{1,0:T(1,128)S(6)} %copy.19.lens, bf16[1,1,256,2048]{3,2,1,0:T(8,128)(2,1)} %q_hbm.1, ...), custom_call_target="tpu_custom_call" | custom-call | flops 2097152000 | bytes 6291456 | tf_op jit(solution)/shard_map/pallas_call | solution.py:323
  31.2 0.0 copy-start.1
  31.2 2.3 %copy.20 = bf16[1,1,256,2048]{3,2,1,0:T(8,128)(2,1)} copy(bf16[1,1,256,2048]{3,2,1,0:T(8,128)(2,1)} %get-tuple-element.10) | data formatting | bytes 2097152
  33.5 0.0 copy-done.1
  33.5 0.0 copy-start
  33.5 0.7 %copy.21 = bf16[1,1,256,512]{3,2,1,0:T(8,128)(2,1)} copy(bf16[1,1,256,512]{3,2,1,0:T(8,128)(2,1)S(1)} %copy-done.1) | data formatting | bytes 524288
  34.2 0.3 copy-done
  34.6 0.0 copy-start.3
  34.6 0.7 %copy.22 = bf16[1,1,256,512]{3,2,1,0:T(8,128)(2,1)} copy(bf16[1,1,256,512]{3,2,1,0:T(8,128)(2,1)S(1)} %copy-done) | data formatting | bytes 524288
  35.3 0.3 copy-done.3
  35.6 0.0 copy-start.2
  35.6 0.7 %copy.23 = bf16[1,8,24,512]{3,2,1,0:T(8,128)(2,1)} copy(bf16[1,8,24,512]{3,2,1,0:T(8,128)(2,1)S(1)} %copy-done.3) | data formatting | bytes 393216
  36.3 0.3 copy-done.2
  36.6 0.7 %copy.24 = bf16[1,8,24,512]{3,2,1,0:T(8,128)(2,1)} copy(bf16[1,8,24,512]{3,2,1,0:T(8,128)(2,1)S(1)} %copy-done.2) | data formatting | bytes 393216
Async XLA Ops:
  31.2 2.4 %copy-start.1 = (bf16[1,1,256,512]{3,2,1,0:T(8,128)(2,1)S(1)}, bf16[1,1,256,512]{3,2,1,0:T(8,128)(2,1)}, u32[]{:S(2)}) copy-start(bf16[1,1,256,512]{3,2,1,0:T(8,128)(2,1)} %get-tuple-element.11) | copy-start | bytes 786436
  33.5 1.0 %copy-start = (bf16[1,1,256,512]{3,2,1,0:T(8,128)(2,1)S(1)}, bf16[1,1,256,512]{3,2,1,0:T(8,128)(2,1)}, u32[]{:S(2)}) copy-start(bf16[1,1,256,512]{3,2,1,0:T(8,128)(2,1)} %get-tuple-element.12) | copy-start | bytes 786436
  34.6 1.0 %copy-start.3 = (bf16[1,8,24,512]{3,2,1,0:T(8,128)(2,1)S(1)}, bf16[1,8,24,512]{3,2,1,0:T(8,128)(2,1)}, u32[]{:S(2)}) copy-start(bf16[1,8,24,512]{3,2,1,0:T(8,128)(2,1)} %get-tuple-element.13) | copy-start | bytes 589828
  35.6 1.0 %copy-start.2 = (bf16[1,8,24,512]{3,2,1,0:T(8,128)(2,1)S(1)}, bf16[1,8,24,512]{3,2,1,0:T(8,128)(2,1)}, u32[]{:S(2)}) copy-start(bf16[1,8,24,512]{3,2,1,0:T(8,128)(2,1)} %get-tuple-element.14) | copy-start | bytes 589828

commit v2 on v1

--- a/solution.py
+++ b/solution.py
@@ -44,11 +44,11 @@
 
 
 def kernel(
-    n, cites, lens, q_hbm, ok_hbm, ov_hbm, go_hbm, pk_hbm, pv_hbm, tab_hbm,
+    n, cites, lens_hbm, q_hbm, ok_hbm, ov_hbm, go_hbm, pk_hbm, pv_hbm, tab_hbm,
     gq, gok, gov, gpk, gpv,
     q, ok, ov, go, pk, pv, tab,
-    tile, tiles_in, sendbuf, fwd_in, backbuf, back_in,
-    stage, gstage, qr, gl, ko, kp, dsp, es, dps, stats, wrow, slot_of, cite_of,
+    lens, cites_in, sendbuf, fwd_in, backbuf, back_in,
+    stage, gstage, qr, gl, ko, kp, dsp, es, dps, stats, wrow, slot_of, cite_of, place_of, bstage,
     load_sem, cs_sem, cr_sem, fs_sem, fr_sem, bs_sem, br_sem,
 ):
     rows = q.shape[0]
@@ -65,7 +65,7 @@
             [
                 (pk_hbm.at[0], pk), (pv_hbm.at[0], pv), (tab_hbm, tab),
                 (ok_hbm.at[0, 0], ok), (ov_hbm.at[0, 0], ov),
-                (q_hbm.at[0, 0], q), (go_hbm.at[0, 0], go),
+                (q_hbm.at[0, 0], q), (go_hbm.at[0, 0], go), (lens_hbm, lens),
             ]
         )
     ]
@@ -80,17 +80,9 @@
     for load in loads:
         load.start()
 
-    lane = lax.broadcasted_iota(jnp.int32, (8, D), 1)
-    wanted = jnp.full((8, D), -1, jnp.int32)
-    for j in range(ncite):
-        wanted = jnp.where(lane == j, cites[0, 0, j], wanted)
-    tile[...] = wanted
-    tiles_in[0] = wanted
-    pl.semaphore_wait(barrier, n - 1)
-
     def ask(k):
         return pltpu.make_async_remote_copy(
-            src_ref=tile, dst_ref=tiles_in.at[k],
+            src_ref=cites.at[0], dst_ref=cites_in.at[k],
             send_sem=cs_sem.at[k], recv_sem=cr_sem.at[k],
             device_id={"enc": lax.rem(me + k, n)}, device_id_type=MESH,
         )
@@ -109,37 +101,22 @@
             device_id={"enc": lax.rem(me + k, n)}, device_id_type=MESH,
         )
 
-    @pl.loop(1, n)
-    def _(k):
-        ask(k).start()
-
-    @pl.loop(0, ncite)
-    def _(j):
-        mine = cites[0, 0, j]
-        owner = lax.div(mine, held)
-
-        def count(i, total):
-            other = cites[0, 0, i]
-            return total + jnp.where((lax.div(other, held) == owner) & (other < mine), 1, 0)
-
-        rank = lax.fori_loop(0, ncite, count, jnp.int32(0))
-        slot_of[j] = lax.rem(owner - me + n, n) * CAP + rank
-
-    @pl.loop(0, n * CAP)
-    def _(s):
-        def find(j, found):
-            return jnp.where(slot_of[j] == s, j, found)
-
-        cite_of[s] = lax.fori_loop(0, ncite, find, jnp.int32(ncite))
-
-    loads[0].wait()
-    loads[1].wait()
+    def unpack(source, target, h):
+        @pl.loop(0, n, unroll=min(n, 4))
+        def _(k):
+            block = source[k, h].astype(F32)
+            for r in range(CAP):
+                target[k * CAP + r, 0] = block[r * plen : (r + 1) * plen]
+                target[k * CAP + r, 1] = block[(CAP + r) * plen : (CAP + r + 1) * plen]
 
     def pick(k, target):
-        own = tiles_in[k] - me * held
-        inside = (own >= 0) & (own < held) & (lane < ncite)
-        low = jnp.min(jnp.where(inside, own, held))
-        high = jnp.max(jnp.where(inside, own, -1))
+        low, high = held, -1
+        for j in range(ncite):
+            asked = cites[0, 0, j] if isinstance(k, int) else cites_in[k, 0, j]
+            own = asked - me * held
+            inside = (own >= 0) & (own < held)
+            low = jnp.minimum(low, jnp.where(inside, own, held))
+            high = jnp.maximum(high, jnp.where(inside, own, -1))
         wrow[k, 0] = low
         wrow[k, 1] = jnp.where(high > low, high, held)
         a = jnp.clip(low, 0, held - 1)
@@ -150,29 +127,38 @@
         for h in range(heads):
             target[k, h] = block[:, h * D : (h + 1) * D]
 
-    @pl.loop(1, n)
-    def _(k):
-        ask(k).wait_recv()
-        pick(k, sendbuf)
-
-    @pl.loop(0, heads)
-    def _(h):
-        @pl.loop(1, n)
-        def _(k):
-            forward(k, h).start()
-
+    @pl.loop(0, ncite)
+    def _(j):
+        mine = cites[0, 0, j]
+        owner = lax.div(mine, held)
+
+        def count(i, total):
+            other = cites[0, 0, i]
+            return total + jnp.where((lax.div(other, held) == owner) & (other < mine), 1, 0)
+
+        rank = lax.fori_loop(0, ncite, count, jnp.int32(0))
+        slot_of[j] = lax.rem(owner - me + n, n) * CAP + rank
+
+    @pl.loop(0, n * CAP)
+    def _(s):
+        def find(j, found):
+            return jnp.where(slot_of[j] == s, j, found)
+
+        cite_of[s] = lax.fori_loop(0, ncite, find, jnp.int32(ncite))
+
+    loads[0].wait()
+    loads[1].wait()
     pick(0, fwd_in)
     for load in loads[2:]:
         load.wait()
 
-    limit = lens[0, 0]
+    limit = lens[0, 0, 0]
     live = lax.broadcasted_iota(jnp.int32, (rows, D), 0) < limit
     causal = lax.broadcasted_iota(jnp.int32, (rows, rows), 0) <= lax.broadcasted_iota(
         jnp.int32, (rows, rows), 1
     )
 
-    @pl.loop(0, heads)
-    def _(h):
+    def own(h):
         own_table = tab[prefix:, :]
         kcols = pl.ds(pl.multiple_of(h * D, D), D)
         key_own = turn(ok[:, kcols].astype(F32), own_table, 1.0).astype(BF16)
@@ -194,21 +180,49 @@
             stats[h, j, 1:2, :] = jnp.sum(weights, axis=0, keepdims=True)
             stats[h, j, 2:3, :] = jnp.sum(weights * gw, axis=0, keepdims=True)
 
+    own(0)
+    pl.semaphore_wait(barrier, n - 1)
+
+    @pl.loop(1, n)
+    def _(k):
+        ask(k).start()
+
+
+    def serve(k):
+        ask(k).wait_recv()
+        pick(k, sendbuf)
+        for h in range(heads):
+            forward(k, h).start()
+
+    @pl.loop(1, n)
+    def _(d):
+        pl.when(me >= d)(lambda: serve(d))
+        pl.when(me + d < n)(lambda: serve(n - d))
+
+    @pl.loop(1, heads)
+    def _(h):
+        own(h)
+
+    @pl.loop(0, held)
+    def _(i):
+        @pl.loop(0, n)
+        def _(k):
+            second = jnp.where(wrow[k, 1] == i, k * CAP + 1, n * CAP)
+            place_of[i, k] = jnp.where(wrow[k, 0] == i, k * CAP, second)
+
+    @pl.loop(1, n)
+    def _(k):
+        ask(k).wait_send()
+
     gstage[ncite] = jnp.zeros(gstage.shape[1:], F32)
 
     @pl.loop(0, heads)
     def _(h):
         @pl.loop(1, n)
         def _(k):
-            forward(k, h).wait_recv()
-
-        @pl.loop(0, n)
-        def _(k):
-            block = fwd_in[k, h].astype(F32)
-            for r in range(CAP):
-                stage[k * CAP + r, 0] = block[r * plen : (r + 1) * plen]
-                stage[k * CAP + r, 1] = block[(CAP + r) * plen : (CAP + r + 1) * plen]
-
+            forward(k, h).wait()
+
+        unpack(fwd_in, stage, h)
         keys = jnp.concatenate([stage[slot_of[j], 0] for j in range(ncite)], axis=0)
         key_pas = turn(keys, tab[:prefix, :], 1.0).astype(BF16)
         kp[h] = key_pas
@@ -255,6 +269,9 @@
 
         give(0, back_in)
 
+    @pl.loop(0, heads)
+    def _(h):
+        key_pas = kp[h]
         kcols = pl.ds(pl.multiple_of(h * D, D), D)
         key_own = ko[h]
         own_table = tab[prefix:, :]
@@ -272,37 +289,32 @@
         gok[0, 0, :, kcols] = turn(own_keys, own_table, -1.0).astype(BF16)
         gov[0, 0, :, kcols] = own_values.astype(BF16)
 
-    for h in range(heads):
+    bstage[n * CAP] = jnp.zeros(bstage.shape[1:], F32)
+
+    @pl.loop(0, heads)
+    def _(h):
         @pl.loop(1, n)
         def _(k):
             back(k, h).wait_recv()
-
-        @pl.loop(0, held)
-        def _(i):
-            def add(k, total):
-                block = back_in[k, h].astype(F32)
-                for r in range(CAP):
-                    hit = wrow[k, r] == i
-                    total = (
-                        total[0] + jnp.where(hit, block[r * plen : (r + 1) * plen], 0.0),
-                        total[1]
-                        + jnp.where(hit, block[(CAP + r) * plen : (CAP + r + 1) * plen], 0.0),
-                    )
-                return total
-
-            zero = jnp.zeros((plen, D), F32)
-            total = lax.fori_loop(0, n, add, (zero, zero))
-            gpk[0, i, :, h * D : (h + 1) * D] = total[0].astype(BF16)
-            gpv[0, i, :, h * D : (h + 1) * D] = total[1].astype(BF16)
-
-    @pl.loop(1, n)
-    def _(k):
-        ask(k).wait_send()
-
-        @pl.loop(0, heads)
-        def _(h):
-            forward(k, h).wait_send()
             back(k, h).wait_send()
+
+        unpack(back_in, bstage, h)
+        kcols = pl.ds(pl.multiple_of(h * D, D), D)
+        for i in range(held):
+            total = bstage[place_of[i, 0]]
+            for k in range(1, n):
+                total += bstage[place_of[i, k]]
+            gpk[0, i, :, kcols] = total[0].astype(BF16)
+            gpv[0, i, :, kcols] = total[1].astype(BF16)
+
+
+def place(*refs):
+    sems = refs[10]
+    copies = [pltpu.make_async_copy(refs[i], refs[5 + i], sems.at[i]) for i in range(5)]
+    for copy in copies:
+        copy.start()
+    for copy in copies:
+        copy.wait()
 
 
 def shards(n, queries, own_keys, own_values, grad_out, pkeys, pvalues, citations, lengths):
@@ -315,15 +327,17 @@
     keys = prefix + rows
     slab = (n, heads, 2 * CAP * plen, D)
     table = jnp.asarray(tables(keys))
-    any_spec = pl.BlockSpec(memory_space=pl.ANY)
+    hbm = pl.BlockSpec(memory_space=pltpu.HBM)
     smem = pl.BlockSpec(memory_space=pltpu.SMEM)
     vmem = pl.BlockSpec(memory_space=pltpu.VMEM)
     like = lambda x: jax.ShapeDtypeStruct(x.shape, x.dtype)
     flops = 2 * 5 * heads * group * rows * keys * D
-    return pl.pallas_call(
+    results = pl.pallas_call(
         functools.partial(kernel, n),
-        out_shape=tuple(like(x) for x in (queries, own_keys, own_values, pkeys, pvalues)),
-        in_specs=[smem] * 2 + [any_spec] * 7,
+        out_shape=tuple(
+            pltpu.VMEM(x.shape, x.dtype) for x in (queries, own_keys, own_values, pkeys, pvalues)
+        ),
+        in_specs=[smem] + [hbm] * 8,
         out_specs=(vmem,) * 5,
         scratch_shapes=[
             pltpu.VMEM((rows, features), BF16),
@@ -333,8 +347,8 @@
             pltpu.VMEM((held, plen, kfeatures), BF16),
             pltpu.VMEM((held, plen, kfeatures), BF16),
             pltpu.VMEM((keys, 2 * D), F32),
-            pltpu.VMEM((8, D), jnp.int32),
-            pltpu.VMEM((n, 8, D), jnp.int32),
+            pltpu.SMEM((1, 1, 1), jnp.int32),
+            pltpu.SMEM((n, 1, ncite), jnp.int32),
             pltpu.VMEM(slab, BF16),
             pltpu.VMEM(slab, BF16),
             pltpu.VMEM(slab, BF16),
@@ -352,7 +366,9 @@
             pltpu.SMEM((n, CAP), jnp.int32),
             pltpu.SMEM((ncite,), jnp.int32),
             pltpu.SMEM((n * CAP,), jnp.int32),
-            pltpu.SemaphoreType.DMA((7,)),
+            pltpu.SMEM((held, n), jnp.int32),
+            pltpu.VMEM((n * CAP + 1, 2, plen, D), F32),
+            pltpu.SemaphoreType.DMA((8,)),
             pltpu.SemaphoreType.DMA((n,)),
             pltpu.SemaphoreType.DMA((n,)),
             pltpu.SemaphoreType.DMA((n, heads)),
@@ -361,12 +377,21 @@
             pltpu.SemaphoreType.DMA((n, heads)),
         ],
         compiler_params=pltpu.CompilerParams(
-            collective_id=0, has_side_effects=True, vmem_limit_bytes=56 * 1024 * 1024
+            collective_id=0, has_side_effects=True, vmem_limit_bytes=61 * 1024 * 1024
         ),
         cost_estimate=pl.CostEstimate(
             flops=flops, bytes_accessed=6 * 1024 * 1024, transcendentals=heads * group * rows * keys
         ),
-    )(citations, lengths, queries, own_keys, own_values, grad_out, pkeys, pvalues, table)
+    )(citations, lengths[None], queries, own_keys, own_values, grad_out, pkeys, pvalues, table)
+    return pl.pallas_call(
+        place,
+        out_shape=tuple(like(x) for x in (queries, own_keys, own_values, pkeys, pvalues)),
+        in_specs=[pl.BlockSpec(memory_space=pl.ANY)] * 5,
+        out_specs=(hbm,) * 5,
+        scratch_shapes=[pltpu.SemaphoreType.DMA((5,))],
+        compiler_params=pltpu.CompilerParams(vmem_limit_bytes=1024 * 1024),
+        cost_estimate=pl.CostEstimate(flops=0, bytes_accessed=2 * 1024 * 1024, transcendentals=0),
+    )(*results)
 
 
 def solution(mesh):

time: 37.5 us -> 30.9 us (0.82)
  local copies, waits for them, and re-layouts: 6.09 us -> 0 us
  Pallas kernels: 29.9 us -> 29.4 us
    unnamed x13 -> x0, local copies, waits for them, and re-layouts: 6.09 us -> none
    pallas_call x1 -> x2, Pallas kernels: 29.9 us -> 29.4 us  [the longest x1 28.1 us: shards(): pl.pallas_call(functools.partial(kernel, n), out_shape=tuple((pltpu.VMEM(...]
where the time goes in v2:
time: 30.9 us; the launch traced here: 30.7 us
  Pallas kernels  29.4 us (95%)
  between operations  1.29 us (4%)
    pallas_call x1, Pallas kernels, shards(): pl.pallas_call(functools.partial(kernel, n), out_shape=tuple((pltpu.VMEM(...  28.1 us
    pallas_call x1, Pallas kernels, shards(): pl.pallas_call(place, out_shape=tuple((like(x) for x in (queries, own_key...  1.31 us

profile of v2, /device:TPU:0, one launch (start us, length us, event | category | flops | bytes accessed | tf_op | source)
XLA Modules:
  0.0 30.7 jit_solution(1669427874429137421)
XLA Ops:
  1.3 28.1 %shard_map.128 = (bf16[1,1,256,2048]{3,2,1,0:T(8,128)(2,1)S(1)}, bf16[1,1,256,512]{3,2,1,0:T(8,128)(2,1)S(1)}, bf16[1,1,256,512]{3,2,1,0:T(8,128)(2,1)S(1)}, bf1...) custom-call(s32[1,1,6]{2,1,0:T(1,128)} %cites.1, s32[1,1,1]{2,1,0:T(1,128)} %bitcast.1.lens_hbm, ...), custom_call_target="tpu_custom_call" | custom-call | flops 2097152000 | bytes 6291456 | tf_op jit(solution)/shard_map/pallas_call | solution.py:335
  29.4 1.3 %shard_map.129 = (bf16[1,1,256,2048]{3,2,1,0:T(8,128)(2,1)}, bf16[1,1,256,512]{3,2,1,0:T(8,128)(2,1)}, bf16[1,1,256,512]{3,2,1,0:T(8,128)(2,1)}, bf16[1,8,24,512]{3,2,1,0:T(8,128)(2,1)}, bf16[1,8,24,512]{3,2,1,0:T(8,128)(2,1)}) custom-call(bf16[1,1,256,2048]{3,2,1,0:T(8,128)(2,1)S(1)} %get-tuple-element.10.refs_0_, ...), custom_call_target="tpu_custom_call" | custom-call | bytes 2097152 | tf_op jit(solution)/shard_map/pallas_call | solution.py:386

commit v3 on v2

--- a/solution.py
+++ b/solution.py
@@ -49,7 +49,7 @@
     q, ok, ov, go, pk, pv, tab,
     lens, cites_in, sendbuf, fwd_in, backbuf, back_in,
     stage, gstage, qr, gl, ko, kp, dsp, es, dps, stats, wrow, slot_of, cite_of, place_of, bstage,
-    load_sem, cs_sem, cr_sem, fs_sem, fr_sem, bs_sem, br_sem,
+    low_sem, high_sem, load_sem, cs_sem, cr_sem, fs_sem, fr_sem, bs_sem, br_sem,
 ):
     rows = q.shape[0]
     heads = ok.shape[1] // D
@@ -71,11 +71,11 @@
     ]
     barrier = pltpu.get_barrier_semaphore()
 
-    @pl.loop(1, n)
-    def _(k):
-        pl.semaphore_signal(
-            barrier, inc=1, device_id={"enc": lax.rem(me + k, n)}, device_id_type=MESH
-        )
+    def tell(sem, neighbour):
+        pl.semaphore_signal(sem, inc=1, device_id={"enc": neighbour}, device_id_type=MESH)
+
+    pl.when(me > 0)(lambda: tell(barrier, me - 1))
+    pl.when(me < n - 1)(lambda: tell(barrier, me + 1))
 
     for load in loads:
         load.start()
@@ -112,7 +112,7 @@
     def pick(k, target):
         low, high = held, -1
         for j in range(ncite):
-            asked = cites[0, 0, j] if isinstance(k, int) else cites_in[k, 0, j]
+            asked = cites[0, 0, j] if isinstance(k, int) and k == 0 else cites_in[k, 0, j]
             own = asked - me * held
             inside = (own >= 0) & (own < held)
             low = jnp.minimum(low, jnp.where(inside, own, held))
@@ -149,6 +149,46 @@
     loads[0].wait()
     loads[1].wait()
     pick(0, fwd_in)
+    def serve(k):
+        ask(k).wait_recv()
+        pick(k, sendbuf)
+        for h in range(2):
+            forward(k, h).start()
+
+    def reach(d):
+        below, above = me >= d, me + d < n
+
+        @pl.when(d > 1)
+        def _():
+            pl.when(below)(lambda: pl.semaphore_wait(low_sem.at[d], 1))
+            pl.when(above)(lambda: pl.semaphore_wait(high_sem.at[d], 1))
+
+        pl.when(below & (me < n - 1))(lambda: tell(low_sem.at[d + 1], me + 1))
+        pl.when(above & (me > 0))(lambda: tell(high_sem.at[d + 1], me - 1))
+        pl.when(below)(lambda: ask(n - d).start())
+        pl.when(above)(lambda: ask(d).start())
+
+    def serve_at(d):
+        pl.when(me >= d)(lambda: serve(d))
+        pl.when(me + d < n)(lambda: serve(n - d))
+
+    pl.semaphore_wait(barrier, jnp.where(me > 0, 1, 0) + jnp.where(me < n - 1, 1, 0))
+    reach(jnp.int32(1))
+
+    @pl.loop(2, n)
+    def _(d):
+        reach(d)
+        serve_at(d - 1)
+
+    serve_at(n - 1)
+
+    @pl.loop(2, heads)
+    def _(h):
+        @pl.loop(1, n)
+        def _(d):
+            pl.when(me >= d)(lambda: forward(d, h).start())
+            pl.when(me + d < n)(lambda: forward(n - d, h).start())
+
     for load in loads[2:]:
         load.wait()
 
@@ -180,26 +220,7 @@
             stats[h, j, 1:2, :] = jnp.sum(weights, axis=0, keepdims=True)
             stats[h, j, 2:3, :] = jnp.sum(weights * gw, axis=0, keepdims=True)
 
-    own(0)
-    pl.semaphore_wait(barrier, n - 1)
-
-    @pl.loop(1, n)
-    def _(k):
-        ask(k).start()
-
-
-    def serve(k):
-        ask(k).wait_recv()
-        pick(k, sendbuf)
-        for h in range(heads):
-            forward(k, h).start()
-
-    @pl.loop(1, n)
-    def _(d):
-        pl.when(me >= d)(lambda: serve(d))
-        pl.when(me + d < n)(lambda: serve(n - d))
-
-    @pl.loop(1, heads)
+    @pl.loop(0, heads)
     def _(h):
         own(h)
 
@@ -368,6 +389,8 @@
             pltpu.SMEM((n * CAP,), jnp.int32),
             pltpu.SMEM((held, n), jnp.int32),
             pltpu.VMEM((n * CAP + 1, 2, plen, D), F32),
+            pltpu.SemaphoreType.REGULAR((n + 1,)),
+            pltpu.SemaphoreType.REGULAR((n + 1,)),
             pltpu.SemaphoreType.DMA((8,)),
             pltpu.SemaphoreType.DMA((n,)),
             pltpu.SemaphoreType.DMA((n,)),

time: 30.9 us -> 29.1 us (0.942)
  Pallas kernels: 29.4 us -> 27.6 us
    pallas_call x1, Pallas kernels: 28.1 us -> 26.3 us  [shards(): pl.pallas_call(functools.partial(kernel, n), out_shape=tuple((pltpu.VMEM(...]
where the time goes in v3:
time: 29.1 us; the launch traced here: 28.9 us
  Pallas kernels  27.6 us (95%)
  between operations  1.29 us (4%)
    pallas_call x1, Pallas kernels, shards(): pl.pallas_call(functools.partial(kernel, n), out_shape=tuple((pltpu.VMEM(...  26.3 us
    pallas_call x1, Pallas kernels, shards(): pl.pallas_call(place, out_shape=tuple((like(x) for x in (queries, own_key...  1.31 us

profile of v3, /device:TPU:0, one launch (start us, length us, event | category | flops | bytes accessed | tf_op | source)
XLA Modules:
  0.0 28.9 jit_solution(5329698040254703296)
XLA Ops:
  1.3 26.3 %shard_map.128 = (bf16[1,1,256,2048]{3,2,1,0:T(8,128)(2,1)S(1)}, bf16[1,1,256,512]{3,2,1,0:T(8,128)(2,1)S(1)}, bf16[1,1,256,512]{3,2,1,0:T(8,128)(2,1)S(1)}, bf1...) custom-call(s32[1,1,6]{2,1,0:T(1,128)} %cites.1, s32[1,1,1]{2,1,0:T(1,128)} %bitcast.1.lens_hbm, ...), custom_call_target="tpu_custom_call" | custom-call | flops 2097152000 | bytes 6291456 | tf_op jit(solution)/shard_map/pallas_call | solution.py:356
  27.6 1.3 %shard_map.129 = (bf16[1,1,256,2048]{3,2,1,0:T(8,128)(2,1)}, bf16[1,1,256,512]{3,2,1,0:T(8,128)(2,1)}, bf16[1,1,256,512]{3,2,1,0:T(8,128)(2,1)}, bf16[1,8,24,512]{3,2,1,0:T(8,128)(2,1)}, bf16[1,8,24,512]{3,2,1,0:T(8,128)(2,1)}) custom-call(bf16[1,1,256,2048]{3,2,1,0:T(8,128)(2,1)S(1)} %get-tuple-element.10.refs_0_, ...), custom_call_target="tpu_custom_call" | custom-call | bytes 2097152 | tf_op jit(solution)/shard_map/pallas_call | solution.py:409

commit v4 on v3

--- a/solution.py
+++ b/solution.py
@@ -186,8 +186,8 @@
     def _(h):
         @pl.loop(1, n)
         def _(d):
-            pl.when(me >= d)(lambda: forward(d, h).start())
-            pl.when(me + d < n)(lambda: forward(n - d, h).start())
+            pl.when(me >= n - d)(lambda: forward(n - d, h).start())
+            pl.when(me + n - d < n)(lambda: forward(d, h).start())
 
     for load in loads[2:]:
         load.wait()
@@ -283,10 +283,14 @@
                 [gstage[a, 0], gstage[b, 0], gstage[a, 1], gstage[b, 1]], axis=0
             ).astype(BF16)
 
-        @pl.loop(1, n)
-        def _(k):
+        def send(k):
             give(k, backbuf)
             back(k, h).start()
+
+        @pl.loop(1, n)
+        def _(d):
+            pl.when(me + n - d < n)(lambda: send(n - d))
+            pl.when(me >= n - d)(lambda: send(d))
 
         give(0, back_in)
 

time: 29.1 us -> 29.2 us (level)
  no operation moved by 1% of the time
where the time goes in v4:
time: 29.2 us; the launch traced here: 29 us
  Pallas kernels  27.7 us (95%)
  between operations  1.29 us (4%)
    pallas_call x1, Pallas kernels, shards(): pl.pallas_call(functools.partial(kernel, n), out_shape=tuple((pltpu.VMEM(...  26.4 us
    pallas_call x1, Pallas kernels, shards(): pl.pallas_call(place, out_shape=tuple((like(x) for x in (queries, own_key...  1.31 us

profile of v4, /device:TPU:0, one launch (start us, length us, event | category | flops | bytes accessed | tf_op | source)
XLA Modules:
  0.0 29.0 jit_solution(16907957597431094355)
XLA Ops:
  1.3 26.4 %shard_map.128 = (bf16[1,1,256,2048]{3,2,1,0:T(8,128)(2,1)S(1)}, bf16[1,1,256,512]{3,2,1,0:T(8,128)(2,1)S(1)}, bf16[1,1,256,512]{3,2,1,0:T(8,128)(2,1)S(1)}, bf1...) custom-call(s32[1,1,6]{2,1,0:T(1,128)} %cites.1, s32[1,1,1]{2,1,0:T(1,128)} %bitcast.1.lens_hbm, ...), custom_call_target="tpu_custom_call" | custom-call | flops 2097152000 | bytes 6291456 | tf_op jit(solution)/shard_map/pallas_call | solution.py:360
  27.7 1.3 %shard_map.129 = (bf16[1,1,256,2048]{3,2,1,0:T(8,128)(2,1)}, bf16[1,1,256,512]{3,2,1,0:T(8,128)(2,1)}, bf16[1,1,256,512]{3,2,1,0:T(8,128)(2,1)}, bf16[1,8,24,512]{3,2,1,0:T(8,128)(2,1)}, bf16[1,8,24,512]{3,2,1,0:T(8,128)(2,1)}) custom-call(bf16[1,1,256,2048]{3,2,1,0:T(8,128)(2,1)S(1)} %get-tuple-element.10.refs_0_, ...), custom_call_target="tpu_custom_call" | custom-call | bytes 2097152 | tf_op jit(solution)/shard_map/pallas_call | solution.py:413
